TPU v7x, 128 devices: a whole 4x4x4 slice. The times are simulated.
128 devices in a mesh: src: 8 (over y, core), rcv: 16 (over x, z).
Axes of the slice: x: 4, y: 4, z: 4, core: 2. Of those that a mesh axis runs over, the one named last changes fastest.
Arguments:
- data: bfloat16 [2, 8192, 8192], P(None, ('src', 'rcv')), may hold values from -0.8984375 to 0.8984375
- fill_mask: int32 [8192, 8192], P(('src', 'rcv')), may hold values 0 or 1
- obliquity: float32 [8192], replicated, may hold values from 0.25 to 4
- aperture: int32 [16, 16, 8], P('src'), may hold values from 0 to 15, as said below
- lengths: int32 [16, 16], P('src', 'rcv'), may hold values from 1 to 8, as said below
Outputs:
- predicted: float32 [2, 8192, 8192], P(None, 'src', 'rcv')
Inputs may be any that keep to these rules, and one draw needn't show every extreme that they name: `aperture`: every entry is a tile index; the 8 entries of one output tile are distinct; only the first lengths entries of a list are used. `lengths`: some output tile uses all 8 entries of its list.
All inputs are finite; a program needn't handle non-finite values. No bound on the sum of `fill_mask` on one device may be relied on, other than what follows from the above.
Results may differ from a plain program's by a relative error of at most 0.0028.
Values may be sent and summed in bfloat16 or wider, within the bound.
A program may use at most 128 MiB of HBM per device.

v0:
```python
import jax
import jax.numpy as jnp
from jax import lax
from jax.sharding import PartitionSpec as P

TILE_SIZE = 512


def complex_product(left_pair, right_pair):
    left_wide = jnp.concatenate([left_pair[0], left_pair[1]], axis=1)
    upper = jnp.concatenate([right_pair[0], right_pair[1]], axis=1)
    lower = jnp.concatenate([-right_pair[1], right_pair[0]], axis=1)
    right_wide = jnp.concatenate([upper, lower], axis=0)
    return jnp.dot(left_wide, right_wide, preferred_element_type=jnp.float32)


def predict_tile(tile_row, my_lists, slot_count, left_piece, column_data):

    def add_slot(slot_index, summed):
        inner_tile = my_lists[tile_row, slot_index]
        left_pair = left_piece(tile_row, slot_index, inner_tile)
        right_pair = lax.dynamic_slice(
            column_data, (0, inner_tile * TILE_SIZE, 0), (2, TILE_SIZE, TILE_SIZE)
        )
        return summed + complex_product(left_pair, right_pair)

    initial = jnp.zeros((TILE_SIZE, 2 * TILE_SIZE), jnp.float32)
    return -lax.fori_loop(0, slot_count, add_slot, initial)


def local(data, fill_mask, obliquity, aperture, lengths):
    local_rows = data.shape[1]
    station_total = data.shape[2]
    src_count = lax.axis_size("src")
    rcv_count = lax.axis_size("rcv")
    devices = src_count * rcv_count
    blocks = data.reshape(2, 1, local_rows, devices, local_rows)
    arrived = lax.all_to_all(blocks, ("src", "rcv"), split_axis=3, concat_axis=1, tiled=True)
    arrived = arrived.reshape(2, devices, local_rows, local_rows)
    transposed = jnp.transpose(arrived, (0, 3, 1, 2)).reshape(2, local_rows, station_total)
    filled = jnp.where(fill_mask[None] == 1, data, transposed)
    tile_block = lax.all_to_all(filled, "rcv", split_axis=2, concat_axis=1, tiled=True)
    span = tile_block.shape[1]
    gains = lax.dynamic_slice_in_dim(obliquity, lax.axis_index("src") * span, span)
    weighted = (tile_block.astype(jnp.float32) * gains[None, :, None]).astype(jnp.bfloat16)
    column_data = lax.all_gather(weighted, "src", axis=1, tiled=True)
    rcv_index = lax.axis_index("rcv")
    my_lists = lax.dynamic_index_in_dim(aperture, rcv_index, 1, keepdims=False)
    tile_rows = span // TILE_SIZE
    row_data = lax.all_gather(tile_block, "rcv", axis=2, tiled=True)

    def left_piece(tile_row, slot_index, inner_tile):
        return lax.dynamic_slice(
            row_data, (0, tile_row * TILE_SIZE, inner_tile * TILE_SIZE), (2, TILE_SIZE, TILE_SIZE)
        )

    results = []
    for tile_row in range(tile_rows):
        results.append(
            predict_tile(tile_row, my_lists, lengths[tile_row, 0], left_piece, column_data)
        )
    stacked = jnp.stack(results).reshape(tile_rows, TILE_SIZE, 2, TILE_SIZE)
    return jnp.transpose(stacked, (2, 0, 1, 3)).reshape(2, tile_rows * TILE_SIZE, TILE_SIZE)


def solution(mesh):
    placed = (
        P(None, ("src", "rcv"), None),
        P(("src", "rcv"), None),
        P(),
        P("src", None, None),
        P("src", "rcv"),
    )
    return jax.shard_map(
        local, mesh=mesh, in_specs=placed, out_specs=P(None, "src", "rcv"), check_vma=False
    )
```

profile of v0, /device:TPU:10, one launch (start us, length us, event | category | flops | bytes accessed | tf_op | source)
XLA Modules:
  0.0 591.6 jit_solution(11816199752961048441)
XLA Ops:
  6.5 6.9 %reshape.25 = bf16[2,1,64,128,64]{4,3,2,0,1:T(8,128)(2,1)} reshape(bf16[2,64,8192]{2,1,0:T(8,128)(2,1)} %param.9) | data formatting | bytes 4194304 | tf_op jit(solution)/shard_map/reshape | solution.py:37
  13.4 6.8 %copy.21 = bf16[2,1,64,128,64]{4,2,0,1,3:T(8,128)(2,1)} copy(bf16[2,1,64,128,64]{4,3,2,0,1:T(8,128)(2,1)} %reshape.25) | data formatting | bytes 4194304 | tf_op jit(solution)/shard_map/reshape | solution.py:37
  20.3 7.6 %reshape.30 = bf16[128,2,4096]{2,1,0:T(2,128)(2,1)} reshape(bf16[128,1,2,64,64]{4,3,2,1,0:T(8,128)(2,1)} %bitcast.58) | data formatting | bytes 4194304
  27.9 10.4 %all-to-all-start = ((bf16[128,2,4096]{2,1,0:T(2,128)(2,1)}), bf16[128,2,4096]{2,1,0:T(2,128)(2,1)S(1)}, u32[]{:S(2)}, u32[]{:S(2)}) async-start(bf16[128,2,4096]{2,1,0:T(2,128)(2,1)} %reshape.30), calls=%async_computation | async-start | bytes 4194304 | tf_op jit(solution)/shard_map/all_to_all | solution.py:38
  38.3 1.9 broadcast_compare_fusion
  40.2 26.6 %all-to-all-done = bf16[128,2,4096]{2,1,0:T(2,128)(2,1)S(1)} async-done(((bf16[128,2,4096]{2,1,0:T(2,128)(2,1)}), bf16[128,2,4096]{2,1,0:T(2,128)(2,1)S(1)}, u32[]{:S(2)}, u32[]{:S(2)}) %all-to-all-start) | async-done | bytes 2097184 | tf_op jit(solution)/shard_map/all_to_all | solution.py:38
  66.8 4.1 reshape.31
  70.9 6.0 %bitcast_bitcast_fusion = bf16[2,64,128,64]{1,3,0,2:T(8,128)(2,1)} fusion(bf16[128,1,2,64,64]{4,3,2,1,0:T(8,128)(2,1)} %reshape.31), kind=kLoop, calls=%fused_computation.46 | loop fusion | bytes 4194304 | tf_op jit(solution)/shard_map/transpose | solution.py:40
  76.9 7.2 %copy.15 = bf16[2,64,128,64]{3,2,1,0:T(8,128)(2,1)} copy(bf16[2,64,128,64]{1,3,0,2:T(8,128)(2,1)} %bitcast_bitcast_fusion) | data formatting | bytes 4194304 | tf_op jit(solution)/shard_map/transpose | solution.py:40
  84.2 6.8 %reshape.27 = bf16[2,64,8192]{2,1,0:T(8,128)(2,1)} reshape(bf16[2,64,128,64]{3,2,1,0:T(8,128)(2,1)} %copy.15) | data formatting | bytes 4194304 | tf_op jit(solution)/shard_map/reshape | solution.py:40
  90.9 3.5 broadcast_select_fusion
  94.4 9.5 %copy.16 = bf16[2,64,8192]{1,0,2:T(2,128)(2,1)} copy(bf16[2,64,8192]{2,1,0:T(8,128)(2,1)} %broadcast_select_fusion) | data formatting | bytes 4194304 | tf_op jit(solution)/shard_map/jit(_where)/select_n | solution.py:41
  103.9 7.5 %reshape.32 = bf16[16,2,32768]{2,1,0:T(2,128)(2,1)} reshape(bf16[8192,2,64]{2,1,0:T(2,128)(2,1)} %bitcast.56) | data formatting | bytes 4194304
  111.4 5.0 all-to-all-start.1
  116.4 26.6 %all-to-all-done.1 = bf16[16,2,32768]{2,1,0:T(2,128)(2,1)S(1)} async-done(((bf16[16,2,32768]{2,1,0:T(2,128)(2,1)}), bf16[16,2,32768]{2,1,0:T(2,128)(2,1)S(1)}, u32[]{:S(2)}, u32[]{:S(2)}) %all-to-all-start.1) | async-done | bytes 2097184 | tf_op jit(solution)/shard_map/all_to_all | solution.py:42
  143.1 4.9 reshape.33
  148.0 9.1 %copy.17 = bf16[2,16,64,512]{3,2,1,0:T(8,128)(2,1)S(1)} copy(bf16[2,16,64,512]{2,0,3,1:T(2,128)(2,1)} %bitcast.57) | data formatting | bytes 4194304 | tf_op jit(solution)/shard_map/all_to_all | solution.py:42
  157.1 2.0 multiply_convert_fusion
  160.7 83.3 %all-gather.5.cloned.1.call-done = bf16[2,8192,512]{2,1,0:T(8,128)(2,1)} async-done(((bf16[2,1024,512]{2,1,0:T(8,128)(2,1)}), bf16[2,8192,512]{2,1,0:T(8,128)(2,1)}) %all-gather.5.cloned.1.call-update) | async-done | bytes 16777232 | tf_op jit(solution)/shard_map/all_gather | solution.py:46
  244.0 209.5 %all-gather.3.cloned.1.call-done = bf16[2,1024,8192]{2,1,0:T(8,128)(2,1)} async-done(((bf16[2,1024,512]{2,1,0:T(8,128)(2,1)}), bf16[2,1024,8192]{2,1,0:T(8,128)(2,1)}) %all-gather.3.cloned.1.call-update) | async-done | bytes 33554448 | tf_op jit(solution)/shard_map/all_gather | solution.py:50
  453.7 58.6 %while.20 = (s32[]{:T(128)}, f32[512,1024]{1,0:T(8,128)S(1)}, s32[]{:T(128)}, s32[2,8]{1,0:T(2,128)S(1)}, bf16[2,1024,8192]{2,1,0:T(8,128)(2,1)}, /*index=5*/bf1...) while((s32[]{:T(128)}, f32[512,1024]{1,0:T(8,128)S(1)}, ...), condition=%wide.region_1.2_spmd, body=%wide.region_0.1_spmd.sunk | while | flops 1085538304 | bytes 11534553 | solution.py:28
  457.2 1.5 dynamic-slice_bitcast_fusion.12
  458.6 1.2 fusion.48
  459.8 1.3 fusion.49
  464.4 1.5 dynamic-slice_bitcast_fusion.12
  465.8 1.2 fusion.48
  467.0 1.3 fusion.49
  471.6 1.5 dynamic-slice_bitcast_fusion.12
  473.1 1.2 fusion.48
  474.2 1.3 fusion.49
  478.8 1.5 dynamic-slice_bitcast_fusion.12
  481.5 1.3 fusion.49
  486.0 1.5 dynamic-slice_bitcast_fusion.12
  488.7 1.3 fusion.49
  493.2 1.5 dynamic-slice_bitcast_fusion.12
  495.9 1.3 fusion.49
  500.5 1.5 dynamic-slice_bitcast_fusion.12
  503.1 1.3 fusion.49
  507.7 1.5 dynamic-slice_bitcast_fusion.12
  510.3 1.3 fusion.49
  512.4 1.5 neg.12
  513.9 3.0 stack.9
  516.9 1.7 copy.18
  518.8 57.4 %while.21 = (s32[]{:T(128)}, f32[512,1024]{1,0:T(8,128)S(1)}, s32[]{:T(128)}, s32[2,8]{1,0:T(2,128)S(1)}, bf16[2,1024,8192]{2,1,0:T(8,128)(2,1)}, /*index=5*/bf1...) while((s32[]{:T(128)}, f32[512,1024]{1,0:T(8,128)S(1)}, ...), condition=%wide.region_3.4_spmd, body=%wide.region_2.3_spmd.sunk | while | flops 1085538304 | bytes 11534553 | solution.py:28
  521.9 1.5 dynamic-slice_bitcast_fusion.13
  523.4 1.2 fusion.53
  524.6 1.3 fusion.54
  529.0 1.5 dynamic-slice_bitcast_fusion.13
  531.7 1.3 fusion.54
  536.1 1.5 dynamic-slice_bitcast_fusion.13
  538.8 1.3 fusion.54
  543.2 1.5 dynamic-slice_bitcast_fusion.13
  545.9 1.3 fusion.54
  550.3 1.5 dynamic-slice_bitcast_fusion.13
  553.0 1.3 fusion.54
  557.4 1.5 dynamic-slice_bitcast_fusion.13
  560.1 1.3 fusion.54
  564.5 1.5 dynamic-slice_bitcast_fusion.13
  567.2 1.3 fusion.54
  571.6 1.5 dynamic-slice_bitcast_fusion.13
  574.3 1.3 fusion.54
  576.2 1.5 neg.13
  577.7 3.0 stack.10
  582.3 2.5 pad_maximum_fusion
  (51 shorter events, 27.1 us)
Async XLA Ops:
  6.5 153.3 %copy-start = (s32[2,16,8]{1,2,0:T(8,128)S(1)}, s32[2,16,8]{1,2,0:T(8,128)}, u32[]{:S(2)}) copy-start(s32[2,16,8]{1,2,0:T(8,128)} %param.12) | copy-start | bytes 3076
  27.9 38.9 %all-to-all-start = ((bf16[128,2,4096]{2,1,0:T(2,128)(2,1)}), bf16[128,2,4096]{2,1,0:T(2,128)(2,1)S(1)}, u32[]{:S(2)}, u32[]{:S(2)}) async-start(bf16[128,2,4096]{2,1,0:T(2,128)(2,1)} %reshape.30), calls=%async_computation | async-start | bytes 4194304 | tf_op jit(solution)/shard_map/all_to_all | solution.py:38
  84.2 6.8 %copy-start.3 = (bf16[2,64,8192]{2,1,0:T(8,128)(2,1)S(1)}, bf16[2,64,8192]{2,1,0:T(8,128)(2,1)}, u32[]{:S(2)}) copy-start(bf16[2,64,8192]{2,1,0:T(8,128)(2,1)} %param.9) | copy-start | bytes 6291460
  111.4 31.7 %all-to-all-start.1 = ((bf16[16,2,32768]{2,1,0:T(2,128)(2,1)}), bf16[16,2,32768]{2,1,0:T(2,128)(2,1)S(1)}, u32[]{:S(2)}, u32[]{:S(2)}) async-start(bf16[16,2,32768]{2,1,0:T(2,128)(2,1)} %reshape.32), calls=%async_computation.1 | async-start | bytes 4194304 | tf_op jit(solution)/shard_map/all_to_all | solution.py:42
  116.4 127.7 %all-gather.5.cloned.1.call-start = ((), (), s32[]{:S(2)}) async-start(), calls=%async_computation.3 | async-start | bytes 18874368 | tf_op jit(solution)/shard_map/all_gather | solution.py:46
  148.0 9.1 %dynamic-slice-start = ((f32[8192]{0:T(1024)}, s32[]{:T(128)}), f32[1024]{0:T(1024)S(1)}, s32[]{:S(2)}) async-start(f32[8192]{0:T(1024)} %param.11, s32[]{:T(128)} %select_n.27), calls=%async_computation.4 | async-start | bytes 8704 | tf_op jit(solution)/shard_map/dynamic_slice | solution.py:44
  157.1 2.0 copy-start.2
  159.1 1.0 copy-start.5
  159.1 294.4 %all-gather.3.cloned.1.call-start = ((), (), s32[]{:S(2)}) async-start(), calls=%async_computation.2 | async-start | bytes 35651584 | tf_op jit(solution)/shard_map/all_gather | solution.py:50
  580.7 1.6 copy-start.4
  582.3 2.5 copy-start.1
Sparse Core Ops, SparseCore 0:
  159.2 84.7 all-gather.4
  246.1 207.2 all-gather.2
where the time goes:
time: 595 us; the launch traced here: 592 us
  waiting for transfers between devices  347 us (58%)
  local copies, waits for them, and re-layouts  111 us (19%)
  loops' own time  43 us (7%)
  other arithmetic  40.8 us (7%)
  matrix products  21.2 us (4%)
  starting transfers between devices  15.5 us (3%)
  between operations  13.5 us (2%)
    all_gather x1, waiting for transfers between devices, local(): row_data = lax.all_gather(tile_block, 'rcv', axis=2, tiled=True)  209 us
    all_gather x1, waiting for transfers between devices, local(): column_data = lax.all_gather(weighted, 'src', axis=1, tiled=True)  83.3 us
    another operation x2, loops' own time, predict_tile(): return -lax.fori_loop(0, slot_count, add_slot, initial)  43 us
    all_to_all x1, waiting for transfers between devices, local(): lax.all_to_all(filled, 'rcv', split_axis=2, concat_axis=1, tiled=True)  26.6 us
    all_to_all x1, waiting for transfers between devices, local(): lax.all_to_all(blocks, ('src', 'rcv'), split_axis=3, concat_axis=1, tiled...  26.6 us
    unnamed x16, local copies, waits for them, and re-layouts  25.4 us
    squeeze x16, local copies, waits for them, and re-layouts, complex_product(): left_wide = jnp.concatenate([left_pair[0], left_pair[1]], axis=1)  23.6 us
    dot_general x16, matrix products, complex_product(): return jnp.dot(left_wide, right_wide, preferred_element_type=jnp.float32)  21.2 us
  transfers between devices with their start and end apart: 4, of which 4 were waited for; matrix products, arithmetic and copies ran while one was open for 0% of the time, Pallas kernels for 0%

commit v1 on v0

v1 whole, which is shorter than its diff:
```python
import jax
import jax.numpy as jnp
from jax import lax
from jax.experimental import pallas as pl
from jax.experimental.pallas import tpu as pltpu
from jax.sharding import PartitionSpec as P

TILE = 512
SLOTS = 8
TILES = 16
ROWS = 64
DEVICES = 128
MESH = pl.DeviceIdType.MESH
F32 = jnp.float32
BF16 = jnp.bfloat16

OFFSET = (0, 3, 1, 2)


def kernel(
    data, mask, gain, lens, aperture,
    out,
    xt, recv, wb, a_out, a0, a1, a2, a3, b0, b1, b2, b3, c_out, c_in, acc, lens_all, lens_s,
    p1_send, p1_recv, l_send, l_recv, l_copy, a2_send, a2_recv, b2_send, b2_recv,
    a3_send, a3_recv, b3_send, b3_recv, s_send, s_recv, c_send, c_recv,
):
    src, rcv = lax.axis_index("src"), lax.axis_index("rcv")
    y, core = src // 2, src % 2
    x, z = rcv // 4, rcv % 4
    me = src * 16 + rcv
    a_bufs = (a0, a1, a2, a3)
    b_bufs = (b0, b1, b2, b3)

    def device(yy, cc, xx, zz):
        return (yy * 2 + cc, xx * 4 + zz)

    def remote(source, target, send, got, to):
        return pltpu.make_async_remote_copy(
            src_ref=source, dst_ref=target, send_sem=send, recv_sem=got,
            device_id=to, device_id_type=MESH,
        )

    lens_all[z] = lens[...]
    length_copies = []
    for k in range(1, 4):
        copy = remote(lens, lens_all.at[z], l_send.at[k - 1], l_recv.at[k - 1],
                      device(y, core, x, (z + k) % 4))
        copy.start()
        length_copies.append(copy)

    def turn(q):
        block = data[:, :, pl.ds(pl.multiple_of(q * 128, 128), 128)].reshape(128, 128)
        xt[pl.ds(q * 2, 2)] = block.T.reshape(2, ROWS, 128)

    def block_copy(target):
        return remote(xt.at[target], recv.at[me], p1_send, p1_recv.at[me // 8],
                      (target // 16, target % 16))

    turn(me // 2)
    own = pltpu.make_async_copy(xt.at[me], recv.at[me], p1_recv.at[me // 8])
    own.start()
    block_copy(me + 1 - 2 * (me % 2)).start()

    @pl.loop(1, 64)
    def _(k):
        q = (me // 2 + k) % 64
        turn(q)
        block_copy(q * 2).start()
        block_copy(q * 2 + 1).start()

    for buf in a_bufs:
        buf[TILES] = jnp.zeros((4, ROWS, 256), BF16)

    lane = lax.broadcasted_iota(jnp.int32, (ROWS, 128), 1)
    low = lane < ROWS
    row = lax.broadcasted_iota(jnp.int32, (ROWS, 128), 0)
    gain_row = jnp.broadcast_to(gain[pl.ds(me // 2, 1), :], (ROWS, 128))
    gains = jnp.sum(
        jnp.where(lane == row + (me % 2) * ROWS, gain_row, 0.0), axis=1, keepdims=True
    )

    def join(first, second):
        return jnp.where(low, first, second)

    def swap(value):
        return pltpu.roll(value, ROWS, 1)

    tile_me = src * 2 + x // 2

    def right_copy(tile):
        to_y = (tile % 4 - z + 4) % 4
        return remote(wb.at[tile], b0.at[tile_me, :, x % 2], b2_send.at[tile], b2_recv.at[y],
                      device(to_y, core, tile // 4, z))

    def is_mine(tile):
        return jnp.logical_and((tile % 4 - z + 4) % 4 == y, tile // 4 == x)

    def right_own(tile):
        return pltpu.make_async_copy(wb.at[tile], b0.at[tile_me, :, x % 2], b2_recv.at[y])

    @pl.loop(0, TILES)
    def _(tile):
        group = recv.at[pl.ds(tile * 8, 8)]
        pltpu.make_async_copy(group, group, p1_recv.at[tile]).wait()
        filled = []
        for q in range(4):
            columns = pl.ds(pl.multiple_of(tile * 512 + q * 128, 128), 128)
            first = recv[tile * 8 + 2 * q].astype(F32)
            second = recv[tile * 8 + 2 * q + 1].astype(F32)
            turned = (join(first, swap(second)), join(swap(first), second))
            keep = mask[:, columns] == 1
            pair = []
            for part in range(2):
                value = jnp.where(keep, data[part, :, columns].astype(F32), turned[part])
                wb[tile, part, :, q * 128:(q + 1) * 128] = (value * gains).astype(BF16)
                pair.append(value)
            filled.append(pair)
        for part in range(2):
            lanes = slice((1 - part) * 128, (2 - part) * 128)
            for half in range(2):
                first, second = filled[half][part], filled[2 + half][part]
                a_out[2 * half, tile, :, lanes] = (-join(first, swap(second))).astype(BF16)
                a_out[2 * half + 1, tile, :, lanes] = (-join(swap(first), second)).astype(BF16)

        @pl.when(is_mine(tile))
        def _():
            right_own(tile).start()

        @pl.when(jnp.logical_not(is_mine(tile)))
        def _():
            right_copy(tile).start()

    pltpu.make_async_copy(a_out.at[z], a0.at[pl.ds(0, TILES), z], a2_recv.at[z]).start()
    left_copies = []
    for k in range(1, 4):
        to = (z + k) % 4
        copy = remote(a_out.at[to], a0.at[pl.ds(0, TILES), z], a2_send.at[k - 1], a2_recv.at[z],
                      device(y, core, x, to))
        copy.start()
        left_copies.append(copy)

    def a_copy(part, from_slot, to_slot, step, index):
        return remote(
            a_bufs[from_slot].at[pl.ds(0, TILES), part],
            a_bufs[to_slot].at[pl.ds(0, TILES), part],
            a3_send.at[index], a3_recv.at[to_slot - 1, part],
            device(y, core, (x + step) % 4, z),
        )

    def b_block(slot, part, which):
        return b_bufs[slot].at[pl.ds(part * 4 + which * 2, 2)]

    def b_copy(part, from_slot, to_slot, step, index):
        return remote(
            b_block(from_slot, part, core), b_block(to_slot, part, core),
            b3_send.at[index], b3_recv.at[to_slot - 1, part],
            device((y + step) % 4, core, x, z),
        )

    def sibling_copy(slot, part):
        return remote(
            b_block(slot, part, core), b_block(slot, part, core),
            s_send.at[slot, part], s_recv.at[slot, part], device(y, 1 - core, x, z),
        )

    def wait_on(ref, sem):
        pltpu.make_async_copy(ref, ref, sem).wait()

    sends = []

    def start(copy):
        copy.start()
        sends.append(copy)

    for part in range(4):
        wait_on(b_block(0, part, core), b2_recv.at[part])
        start(b_copy(part, 0, 1, 1, part))
        start(b_copy(part, 0, 2, 3, 4 + part))
        start(sibling_copy(0, part))
        wait_on(a0.at[pl.ds(0, TILES), part], a2_recv.at[part])
        start(a_copy(part, 0, 1, 1, part))
        start(a_copy(part, 0, 2, 3, 4 + part))

    for k in range(1, 4):
        length_copies[k - 1].wait_recv()
    pltpu.make_async_copy(lens_all, lens_s, l_copy).start()
    pltpu.make_async_copy(lens_all, lens_s, l_copy).wait()

    def unit(a_slot, b_slot):
        a_buf, b_buf = a_bufs[a_slot], b_bufs[b_slot]
        piece = (x + OFFSET[a_slot]) % 4
        column = (y + OFFSET[b_slot] + z) % 4
        used = lens_s[column, piece // 2, 0]

        def product(slot):
            inner = aperture[piece // 2, x * 4 + column, slot]
            left = a_buf[jnp.where(slot < used, inner, TILES)].reshape(256, 256)
            right = b_buf[inner].reshape(256, 512)
            upper = jnp.concatenate([left[:, 128:], -left[:, :128]], axis=1)
            wide = jnp.concatenate([upper, left], axis=0)
            return jnp.dot(wide, right, preferred_element_type=F32)

        acc[...] = product(0)

        @pl.loop(1, SLOTS)
        def _(slot):
            acc[...] += product(slot)

        mine = column == z

        @pl.when(mine)
        def _():
            out[:, pl.ds(pl.multiple_of(piece * 256, 256), 256), :] = acc[...].reshape(2, 256, TILE)

        @pl.when(jnp.logical_not(mine))
        def _():
            c_out[a_slot, b_slot] = acc[...].reshape(2, 256, TILE).astype(BF16)
            result_copy(a_slot, b_slot).start()

    def result_copy(a_slot, b_slot):
        piece = (x + OFFSET[a_slot]) % 4
        column = (y + OFFSET[b_slot] + z) % 4
        behind = (z - column + 4) % 4 - 1
        return remote(
            c_out.at[a_slot, b_slot], c_in.at[behind, piece],
            c_send.at[a_slot, b_slot], c_recv.at[behind, piece], device(y, core, x, column),
        )

    for part in range(4):
        sibling_copy(0, part).wait_recv()
    unit(0, 0)

    def wait_a(slot, part):
        wait_on(a_bufs[slot].at[pl.ds(0, TILES), part], a3_recv.at[slot - 1, part])

    def wait_b(slot, part):
        wait_on(b_block(slot, part, core), b3_recv.at[slot - 1, part])

    for part in range(4):
        for slot in (1, 2):
            forward = part // 2 == slot - 1
            step = 1 if slot == 1 else 3
            wait_b(slot, part)
            if forward:
                start(b_copy(part, slot, 3, step, 8 + part))
            start(sibling_copy(slot, part))
            wait_a(slot, part)
            if forward:
                start(a_copy(part, slot, 3, step, 8 + part))
    for slot in (1, 2):
        for part in range(4):
            sibling_copy(slot, part).wait_recv()
    for pair in ((1, 0), (0, 1), (1, 1), (2, 0), (0, 2), (2, 1), (1, 2), (2, 2)):
        unit(*pair)
    for part in range(4):
        wait_b(3, part)
        start(sibling_copy(3, part))
    for part in range(4):
        wait_a(3, part)
        sibling_copy(3, part).wait_recv()
    for pair in ((3, 0), (0, 3), (3, 1), (1, 3), (3, 2), (2, 3), (3, 3)):
        unit(*pair)

    for piece in range(4):
        for behind in range(3):
            wait_on(c_in.at[behind, piece], c_recv.at[behind, piece])

        @pl.loop(0, 8)
        def _(step):
            rows = pl.ds(pl.multiple_of(step * 32, 32), 32)
            target = pl.ds(pl.multiple_of(piece * 256 + step * 32, 32), 32)
            total = out[:, target, :]
            for behind in range(3):
                total += c_in[behind, piece, :, rows, :].astype(F32)
            out[:, target, :] = total

    sent = xt.at[pl.ds(0, DEVICES - 1)]
    pltpu.make_async_copy(sent, sent, p1_send).wait()
    for copy in length_copies + left_copies + sends:
        copy.wait_send()

    @pl.loop(0, TILES)
    def _(tile):
        @pl.when(jnp.logical_not(is_mine(tile)))
        def _():
            right_copy(tile).wait_send()

    for a_slot in range(4):
        for b_slot in range(4):
            @pl.when((y + OFFSET[b_slot]) % 4 != 0)
            def _():
                result_copy(a_slot, b_slot).wait_send()


def local(data, fill_mask, obliquity, aperture, lengths):
    vmem = pl.BlockSpec(memory_space=pltpu.VMEM)
    dma = pltpu.SemaphoreType.DMA
    lens = jnp.pad(jnp.broadcast_to(lengths, (2, 128)), ((0, 6), (0, 0)))
    return pl.pallas_call(
        kernel,
        out_shape=jax.ShapeDtypeStruct((2, 2 * TILE, TILE), F32),
        in_specs=[vmem, vmem, vmem, vmem, pl.BlockSpec(memory_space=pltpu.SMEM)],
        out_specs=vmem,
        scratch_shapes=[
            pltpu.VMEM((DEVICES, ROWS, 128), BF16),
            pltpu.VMEM((DEVICES, ROWS, 128), BF16),
            pltpu.VMEM((TILES, 2, ROWS, TILE), BF16),
            pltpu.VMEM((4, TILES, ROWS, 256), BF16),
        ]
        + [pltpu.VMEM((TILES + 1, 4, ROWS, 256), BF16)] * 4
        + [pltpu.VMEM((TILES, 2, 2, ROWS, TILE), BF16)] * 4
        + [
            pltpu.VMEM((4, 4, 2, 256, TILE), BF16),
            pltpu.VMEM((3, 4, 2, 256, TILE), BF16),
            pltpu.VMEM((TILE, TILE), F32),
            pltpu.VMEM((4, 8, 128), jnp.int32),
            pltpu.SMEM((4, 8, 128), jnp.int32),
            dma(()), dma((16,)), dma((3,)), dma((3,)), dma(()), dma((3,)), dma((4,)), dma((16,)), dma((4,)),
            dma((12,)), dma((3, 4)), dma((12,)), dma((3, 4)), dma((4, 4)), dma((4, 4)), dma((4, 4)), dma((3, 4)),
        ],
        compiler_params=pltpu.CompilerParams(
            has_side_effects=True, vmem_limit_bytes=63 * 1024 * 1024
        ),
        cost_estimate=pl.CostEstimate(
            flops=17_000_000_000, bytes_accessed=10_000_000, transcendentals=0
        ),
    )(data, fill_mask, obliquity.reshape(64, 128), lens, aperture)


def solution(mesh):
    placed = (
        P(None, ("src", "rcv"), None),
        P(("src", "rcv"), None),
        P(),
        P("src", None, None),
        P("src", "rcv"),
    )
    return jax.shard_map(
        local, mesh=mesh, in_specs=placed, out_specs=P(None, "src", "rcv"), check_vma=False
    )
```

time: 595 us -> 251 us (0.42)
  the two profiles are of different devices: /device:TPU:10 before, /device:TPU:1 now
where the time goes in v1:
time: 251 us
  Pallas kernels  243 us (97%)
  local copies, waits for them, and re-layouts  7.34 us (3%)
    pallas_call x1, Pallas kernels, local(): pl.pallas_call(kernel, out_shape=jax.ShapeDtypeStruct((2, 2 * TILE, TILE)...  243 us
    unnamed x2, local copies, waits for them, and re-layouts  6.02 us

profile of v1, /device:TPU:1, one launch (start us, length us, event | category | flops | bytes accessed | tf_op | source)
XLA Modules:
  0.0 250.6 jit_solution(15242819212689929260)
XLA Ops:
  0.0 0.7 pad.6
  0.7 0.7 pad.7.lens
  1.3 1.4 copy.6.aperture
  2.7 243.3 %shard_map.55 = f32[2,1024,512]{2,1,0:T(8,128)} custom-call(bf16[2,64,8192]{2,1,0:T(8,128)(2,1)} %data.1, s32[64,8192]{1,0:T(8,128)} %mask.1, f32[64,128]{1,0:T(8,128)} %bitcast.2, s32[8,128]{1,0:T(8,128)} %pad.7.lens, s32[2,16,8]{2,1,0:T(8,128)} %copy.6.aperture), custom_call_target="tpu_custom_call" | custom-call | flops 16999999488 | bytes 10000000 | tf_op jit(solution)/shard_map/pallas_call | solution.py:299
  246.0 4.6 %copy.8 = f32[2,1024,512]{2,1,0:T(8,128)} copy(f32[2,1024,512]{2,1,0:T(8,128)} %shard_map.55) | data formatting | bytes 8388608

commit v2 on v0

v2 whole, which is shorter than its diff:
```python
import jax
import jax.numpy as jnp
from jax import lax
from jax.experimental import pallas as pl
from jax.experimental.pallas import tpu as pltpu
from jax.sharding import PartitionSpec as P

TILE = 512
SLOTS = 8
TILES = 16
ROWS = 64
DEVICES = 128
MESH = pl.DeviceIdType.MESH
F32 = jnp.float32
BF16 = jnp.bfloat16


def kernel(
    data, mask, gain, lens, aperture,
    c_in,
    xt, recv, wb, a_out, a0, a1, a2, a3, b0, b1, b2, b3, c_out, lens_own, lens_all, lens_s, lists,
    p1_send, p1_recv, l_send, l_recv, l_copy, a2_send, a2_recv, b2_send, b2_recv,
    a3_send, a3_recv, b3_send, b3_recv, s_send, s_recv, c_send, c_recv,
):
    src, rcv = lax.axis_index("src"), lax.axis_index("rcv")
    y, core = src // 2, src % 2
    x, z = rcv // 4, rcv % 4
    me = src * 16 + rcv
    lefts = (a0, a1, a2, a3)
    rights = (b0, b1, b2, b3)

    def device(yy, cc, xx, zz):
        return (yy * 2 + cc, xx * 4 + zz)

    def remote(source, target, send, got, to):
        return pltpu.make_async_remote_copy(
            src_ref=source, dst_ref=target, send_sem=send, recv_sem=got,
            device_id=to, device_id_type=MESH,
        )

    def wait_on(ref, sem):
        pltpu.make_async_copy(ref, ref, sem).wait()

    list_copy = pltpu.make_async_copy(aperture, lists, l_copy.at[0])
    list_copy.start()

    eye = (
        lax.broadcasted_iota(jnp.int32, (256, 256), 0)
        == lax.broadcasted_iota(jnp.int32, (256, 256), 1)
    ).astype(F32).astype(BF16)

    def turn(q):
        block = data[:, :, pl.ds(pl.multiple_of(q * 256, 256), 256)].reshape(128, 256)
        turned = lax.dot_general(
            eye, block, (((1,), (1,)), ((), ())), preferred_element_type=F32
        )
        xt[pl.ds(q * 4, 4)] = turned.astype(BF16).reshape(4, ROWS, 128)

    def block_copy(target):
        return remote(xt.at[target], recv.at[me], p1_send, p1_recv.at[me // 8],
                      (target // 16, target % 16))

    turn(me // 4)
    pltpu.make_async_copy(xt.at[me], recv.at[me], p1_recv.at[me // 8]).start()
    for i in range(1, 4):
        block_copy(me // 4 * 4 + (me + i) % 4).start()

    @pl.loop(1, 32)
    def _(k):
        q = (me // 4 + k) % 32
        turn(q)
        for i in range(4):
            block_copy(q * 4 + (me + i) % 4).start()

    lens_own[0:1, :] = jnp.broadcast_to(lens[:, 0:1], (1, 128))
    lens_own[1:2, :] = jnp.broadcast_to(lens[:, 1:2], (1, 128))
    lens_own[2:8, :] = jnp.zeros((6, 128), jnp.int32)
    lens_all[z] = lens_own[...]
    length_copies = []
    for k in range(1, 4):
        copy = remote(lens_own, lens_all.at[z], l_send.at[k - 1], l_recv.at[k - 1],
                      device(y, core, x, (z + k) % 4))
        copy.start()
        length_copies.append(copy)

    for buf in lefts:
        for e in range(2):
            buf[e, TILES] = jnp.zeros((4, 32, 256), BF16)

    lane = lax.broadcasted_iota(jnp.int32, (ROWS, 128), 1)
    low = lane < ROWS
    row = lax.broadcasted_iota(jnp.int32, (ROWS, 128), 0)
    gain_row = jnp.broadcast_to(gain[pl.ds(me // 2, 1), :], (ROWS, 128))
    gains = jnp.sum(
        jnp.where(lane == row + (me % 2) * ROWS, gain_row, 0.0), axis=1, keepdims=True
    )

    def join(first, second):
        return jnp.where(low, first, second)

    def swap(value):
        return pltpu.roll(value, ROWS, 1)

    @pl.loop(0, TILES)
    def _(step):
        tile = (me // 8 - step - 1 + x % 2 + TILES) % TILES
        group = recv.at[pl.ds(tile * 8, 8)]
        wait_on(group, p1_recv.at[tile])
        filled = []
        for q in range(4):
            columns = pl.ds(pl.multiple_of(tile * 512 + q * 128, 128), 128)
            first = recv[tile * 8 + 2 * q].astype(F32)
            second = recv[tile * 8 + 2 * q + 1].astype(F32)
            turned = (join(first, swap(second)), join(swap(first), second))
            keep = mask[:, columns] == 1
            pair = []
            for part in range(2):
                value = jnp.where(keep, data[part, :, columns].astype(F32), turned[part])
                weighted = (value * gains).astype(BF16)
                wb[tile, q // 2, part, :, q % 2 * 128:(q % 2 + 1) * 128] = weighted
                pair.append(value)
            filled.append(pair)
        for part in range(2):
            lanes = slice((1 - part) * 128, (2 - part) * 128)
            for half in range(2):
                first, second = filled[half][part], filled[2 + half][part]
                for odd, value in ((0, join(first, swap(second))), (1, join(swap(first), second))):
                    value = (-value).astype(BF16)
                    a_out[2 * half + odd, 0, tile, :, lanes] = value[:32]
                    a_out[2 * half + odd, 1, tile, :, lanes] = value[32:]

        d = (z - tile % 4 + 4) % 4
        for h in range(2):
            to_y = 2 * (d % 2) + h
            source = wb.at[tile, h]
            target = b0.at[d // 2, y, core, x // 2, :, x % 2]
            mine = jnp.logical_and(to_y == y, tile // 4 == x)

            @pl.when(mine)
            def _():
                pltpu.make_async_copy(source, target, b2_recv.at[d // 2]).start()

            @pl.when(jnp.logical_not(mine))
            def _():
                remote(source, target, b2_send, b2_recv.at[d // 2],
                       device(to_y, core, tile // 4, z)).start()
        for k in range(1, 4):
            to = (z + k) % 4
            for e in range(2):
                remote(a_out.at[to, e, tile], a0.at[e, tile, z], a2_send, a2_recv.at[e, z],
                       device(y, core, x, to)).start()

    for e in range(2):
        pltpu.make_async_copy(
            a_out.at[z, e], a0.at[e, pl.ds(0, TILES), z], a2_recv.at[e, z]
        ).start()

    def left_half(stage, e):
        return lefts[stage].at[e, pl.ds(0, TILES)]

    def right_half(stage, e):
        return rights[stage].at[e, :, core]

    def source_of(stage, e):
        return (0, e) if stage == 1 else (0, 1 - e) if stage == 2 else (1, e)

    def left_copy(stage, e):
        return remote(
            left_half(*source_of(stage, e)), left_half(stage, e),
            a3_send.at[stage - 1, e], a3_recv.at[stage - 1, e],
            device(y, core, (x + 1 + 2 * e) % 4, z),
        )

    def right_copy(stage, e):
        return remote(
            right_half(*source_of(stage, e)), right_half(stage, e),
            b3_send.at[stage - 1, e], b3_recv.at[stage - 1, e],
            device((y + 1 + 2 * e) % 4, core, x, z),
        )

    def sibling_copy(stage, e):
        return remote(
            right_half(stage, e), right_half(stage, e),
            s_send.at[stage, e], s_recv.at[stage, e], device(y, 1 - core, x, z),
        )

    def offset(stage, e):
        return 0 if stage == 0 else 2 if stage == 3 else 3 - 2 * e

    def half_of(stage, e):
        return 1 - e if stage == 2 else e

    def units(left_stage, right_stage):
        @pl.loop(0, 4)
        def _(step):
            ea, eb = step // 2, step % 2
            piece = (x + offset(left_stage, ea)) % 4
            half = half_of(left_stage, ea)
            yy = (y + offset(right_stage, eb)) % 4
            d = 2 * half_of(right_stage, eb) + yy // 2
            column = (z - d + 4) % 4
            used = lens_s[column, piece // 2, 0]
            total = None
            for slot in range(SLOTS):
                inner = lists[piece // 2, slot, x * 4 + column]
                left = lefts[left_stage][ea, jnp.where(slot < used, inner, TILES)].reshape(128, 256)
                right = rights[right_stage][eb, inner // 4, inner // 2 % 2, inner % 2].reshape(256, 256)
                upper = jnp.concatenate([left[:, 128:], -left[:, :128]], axis=1)
                wide = jnp.concatenate([upper, left], axis=0)
                term = jnp.dot(wide, right, preferred_element_type=F32)
                total = term if total is None else total + term
            place = (left_stage * 4 + right_stage) * 4 + step
            c_out[place] = total.astype(BF16).reshape(2, 4, 32, 256)
            columns = pl.ds(pl.multiple_of(yy % 2 * 256, 256), 256)
            target = c_in.at[d, :, piece, :, half, :, columns]

            @pl.when(d == 0)
            def _():
                pltpu.make_async_copy(c_out.at[place], target, c_recv.at[0]).start()

            @pl.when(d != 0)
            def _():
                remote(c_out.at[place], target, c_send, c_recv.at[d],
                       device(y, core, x, column)).start()

    for e in range(2):
        wait_on(right_half(0, e), b2_recv.at[e])
        right_copy(1, e).start()
        sibling_copy(0, e).start()
    for e in range(2):
        for part in range(4):
            wait_on(a0.at[e, pl.ds(0, TILES), part], a2_recv.at[e, part])
        left_copy(1, e).start()
    for e in range(2):
        right_copy(2, e).start()
        left_copy(2, e).start()

    for k in range(1, 4):
        length_copies[k - 1].wait_recv()
    pltpu.make_async_copy(lens_all, lens_s, l_copy.at[1]).start()
    pltpu.make_async_copy(lens_all, lens_s, l_copy.at[1]).wait()
    list_copy.wait()

    for e in range(2):
        sibling_copy(0, e).wait_recv()
    units(0, 0)
    for stage in range(1, 4):
        for e in range(2):
            wait_on(right_half(stage, e), b3_recv.at[stage - 1, e])
            sibling_copy(stage, e).start()
            if stage == 1:
                right_copy(3, e).start()
        for e in range(2):
            wait_on(left_half(stage, e), a3_recv.at[stage - 1, e])
            if stage == 1:
                left_copy(3, e).start()
        for earlier in range(stage):
            units(stage, earlier)
        for e in range(2):
            sibling_copy(stage, e).wait_recv()
        for earlier in range(stage + 1):
            units(earlier, stage)

    wait_on(xt.at[pl.ds(0, DEVICES - 1)], p1_send)
    wait_on(wb.at[pl.ds(0, TILES - 1)], b2_send)
    wait_on(a_out.at[pl.ds(0, 3)], a2_send)
    for copy in length_copies:
        copy.wait_send()
    for e in range(2):
        for stage in range(4):
            sibling_copy(stage, e).wait_send()
        for stage in range(1, 4):
            left_copy(stage, e).wait_send()
            right_copy(stage, e).wait_send()
    wait_on(c_out.at[pl.ds(0, 48)], c_send)
    for d in range(4):
        wait_on(c_in.at[d], c_recv.at[d])


def local(data, fill_mask, obliquity, aperture, lengths):
    vmem = pl.BlockSpec(memory_space=pltpu.VMEM)
    far = pl.BlockSpec(memory_space=pl.ANY)
    dma = pltpu.SemaphoreType.DMA
    sums = pl.pallas_call(
        kernel,
        out_shape=jax.ShapeDtypeStruct((4, 2, 4, 4, 2, 32, TILE), BF16),
        in_specs=[vmem, vmem, vmem, vmem, far],
        out_specs=far,
        scratch_shapes=[
            pltpu.VMEM((DEVICES, ROWS, 128), BF16),
            pltpu.VMEM((DEVICES, ROWS, 128), BF16),
            pltpu.VMEM((TILES, 2, 2, ROWS, 256), BF16),
            pltpu.VMEM((4, 2, TILES, 32, 256), BF16),
        ]
        + [pltpu.VMEM((2, TILES + 1, 4, 32, 256), BF16)] * 4
        + [pltpu.VMEM((2, 4, 2, 2, 2, 2, ROWS, 256), BF16)] * 4
        + [
            pltpu.VMEM((64, 2, 4, 32, 256), BF16),
            pltpu.VMEM((8, 128), jnp.int32),
            pltpu.VMEM((4, 8, 128), jnp.int32),
            pltpu.SMEM((4, 8, 128), jnp.int32),
            pltpu.SMEM((2, SLOTS, TILES), jnp.int32),
            dma(()), dma((16,)), dma((3,)), dma((3,)), dma((2,)), dma(()), dma((2, 4)), dma(()), dma((2,)),
            dma((3, 2)), dma((3, 2)), dma((3, 2)), dma((3, 2)), dma((4, 2)), dma((4, 2)), dma(()), dma((4,)),
        ],
        compiler_params=pltpu.CompilerParams(
            has_side_effects=True, vmem_limit_bytes=63 * 1024 * 1024
        ),
        cost_estimate=pl.CostEstimate(
            flops=17_000_000_000, bytes_accessed=12_000_000, transcendentals=0
        ),
    )(data, fill_mask, obliquity.reshape(64, 128), lengths.T, jnp.swapaxes(aperture, 1, 2))
    total = sums[0].astype(F32)
    for d in range(1, 4):
        total = total + sums[d].astype(F32)
    return total.reshape(2, 2 * TILE, TILE)


def solution(mesh):
    placed = (
        P(None, ("src", "rcv"), None),
        P(("src", "rcv"), None),
        P(),
        P("src", None, None),
        P("src", "rcv"),
    )
    return jax.shard_map(
        local, mesh=mesh, in_specs=placed, out_specs=P(None, "src", "rcv"), check_vma=False
    )
```

time: 595 us -> 206 us (0.35)
  waiting for transfers between devices: 347 us -> 0 us
  Pallas kernels: 0 us -> 199 us
  local copies, waits for them, and re-layouts: 111 us -> 0 us
  loops' own time: 43 us -> 0 us
  other arithmetic: 40.8 us -> 7.22 us
  matrix products: 21.2 us -> 0 us
  starting transfers between devices: 15.5 us -> 0 us
  between operations: 13.5 us -> 0.01 us
    all_gather x2 -> x0, waiting for transfers between devices: 293 us -> none  [the longest x1 209 us: local(): row_data = lax.all_gather(tile_block, 'rcv', axis=2, tiled=True)]
    pallas_call x0 -> x1, Pallas kernels: none -> 199 us  [local(): pl.pallas_call(kernel, out_shape=jax.ShapeDtypeStruct((4, 2, 4, 4, 2, 32,...]
    all_to_all x2 -> x0, waiting for transfers between devices: 53.2 us -> none  [the longest x1 26.6 us: local(): lax.all_to_all(filled, 'rcv', split_axis=2, concat_axis=1, tiled=True)]
    another operation x2 -> x0, loops' own time: 43 us -> none  [predict_tile(): return -lax.fori_loop(0, slot_count, add_slot, initial)]
    unnamed x16 -> x0, local copies, waits for them, and re-layouts: 25.4 us -> none
    squeeze x16 -> x0, local copies, waits for them, and re-layouts: 23.6 us -> none  [complex_product(): left_wide = jnp.concatenate([left_pair[0], left_pair[1]], axis=1)]
    neg x18 -> x0, other arithmetic: 21.7 us -> none  [the longest x16 18.7 us: complex_product(): lower = jnp.concatenate([-right_pair[1], right_pair[0]], axis=1)]
    dot_general x16 -> x0, matrix products: 21.2 us -> none  [complex_product(): return jnp.dot(left_wide, right_wide, preferred_element_type=jnp.float32)]
  transfers between devices with their start and end apart: 4 -> 0, of which waited for: 4 -> 0; matrix products, arithmetic and copies ran while one was open for 0% -> 0% of each run, Pallas kernels for 0% -> 0%
where the time goes in v2:
time: 206 us
  Pallas kernels  199 us (97%)
  other arithmetic  7.22 us (4%)
    pallas_call x1, Pallas kernels, local(): pl.pallas_call(kernel, out_shape=jax.ShapeDtypeStruct((4, 2, 4, 4, 2, 32,...  199 us
    add x1, other arithmetic, local(): total = total + sums[d].astype(F32)  7.22 us

profile of v2, /device:TPU:10, one launch (start us, length us, event | category | flops | bytes accessed | tf_op | source)
XLA Modules:
  0.0 206.0 jit_solution(18174264814608751049)
XLA Ops:
  0.0 198.7 %shard_map.55 = bf16[4,2,4,4,2,32,512]{6,5,4,3,2,1,0:T(8,128)(2,1)} custom-call(bf16[2,64,8192]{2,1,0:T(8,128)(2,1)} %data.1, s32[64,8192]{1,0:T(8,128)} %mask.1, f32[64,128]{1,0:T(8,128)} %bitcast.4, s32[1,2]{1,0:T(1,128)} %bitcast.6, s32[2,8,16]{2,1,0:T(8,128)} %bitcast.5), custom_call_target="tpu_custom_call" | custom-call | flops 16999999488 | bytes 12000000 | tf_op jit(solution)/shard_map/pallas_call | solution.py:284
  198.7 7.2 %convert_add_fusion = f32[1,2,4,4,2,32,512]{6,5,4,3,2,1,0:T(8,128)} fusion(bf16[4,2,4,4,2,32,512]{6,5,4,3,2,1,0:T(8,128)(2,1)} %shard_map.55), kind=kLoop, calls=%fused_computation | loop fusion | flops 7340032 | bytes 12582912 | tf_op jit(solution)/shard_map/add | solution.py:315

commit v3 on v2

--- a/solution.py
+++ b/solution.py
@@ -16,11 +16,11 @@
 
 
 def kernel(
-    data, mask, gain, lens, aperture,
+    data_far, mask_far, gain, lens, aperture,
     c_in,
-    xt, recv, wb, a_out, a0, a1, a2, a3, b0, b1, b2, b3, c_out, lens_own, lens_all, lens_s, lists,
+    data, mask, xt, recv, wb, a_out, a0, a1, a2, a3, b0, b1, b2, b3, c_out, lens_own, lens_all, lens_s, lists,
     p1_send, p1_recv, l_send, l_recv, l_copy, a2_send, a2_recv, b2_send, b2_recv,
-    a3_send, a3_recv, b3_send, b3_recv, s_send, s_recv, c_send, c_recv,
+    a3_send, a3_recv, b3_send, b3_recv, s_send, s_recv, c_send, c_recv, in_copy, met,
 ):
     src, rcv = lax.axis_index("src"), lax.axis_index("rcv")
     y, core = src // 2, src % 2
@@ -41,26 +41,49 @@
     def wait_on(ref, sem):
         pltpu.make_async_copy(ref, ref, sem).wait()
 
+    data_copy = pltpu.make_async_copy(data_far, data, in_copy.at[0])
+    mask_copy = pltpu.make_async_copy(mask_far, mask, in_copy.at[1])
     list_copy = pltpu.make_async_copy(aperture, lists, l_copy.at[0])
+    data_copy.start()
+    mask_copy.start()
     list_copy.start()
 
-    eye = (
-        lax.broadcasted_iota(jnp.int32, (256, 256), 0)
-        == lax.broadcasted_iota(jnp.int32, (256, 256), 1)
-    ).astype(F32).astype(BF16)
-
-    def turn(q):
-        block = data[:, :, pl.ds(pl.multiple_of(q * 256, 256), 256)].reshape(128, 256)
-        turned = lax.dot_general(
-            eye, block, (((1,), (1,)), ((), ())), preferred_element_type=F32
-        )
-        xt[pl.ds(q * 4, 4)] = turned.astype(BF16).reshape(4, ROWS, 128)
+    barrier = pltpu.get_barrier_semaphore()
+    along_x = [device(y, core, (x + k) % 4, z) for k in range(1, 4)]
+    along_y = [device((y + k) % 4, core, x, z) for k in range(1, 4)]
+    along_z = [device(y, core, x, (z + k) % 4) for k in range(1, 4)]
+    sibling = [device(y, 1 - core, x, z)]
+
+    def tell(semaphore, others):
+        for other in others:
+            pl.semaphore_signal(semaphore, inc=1, device_id=other, device_id_type=MESH)
+
+    def turn(first, last):
+        @pl.loop(first, last)
+        def _(step):
+            for i in range(2):
+                q = step * 2 + i
+                block = data[:, :, pl.ds(pl.multiple_of(q * 256, 256), 256)].reshape(128, 256)
+                xt[pl.ds(q * 4, 4)] = block.T.reshape(4, ROWS, 128)
+
+    tell(barrier, along_x + along_y + along_z + sibling)
+    data_copy.wait()
+    turn(0, 4)
+    pl.semaphore_wait(barrier, 10)
+    tell(met.at[0], along_x)
+    turn(4, 8)
+    pl.semaphore_wait(met.at[0], 3)
+    tell(met.at[1], along_y)
+    turn(8, 12)
+    pl.semaphore_wait(met.at[1], 3)
+    tell(met.at[2], sibling)
+    turn(12, 16)
+    pl.semaphore_wait(met.at[2], 1)
 
     def block_copy(target):
         return remote(xt.at[target], recv.at[me], p1_send, p1_recv.at[me // 8],
                       (target // 16, target % 16))
 
-    turn(me // 4)
     pltpu.make_async_copy(xt.at[me], recv.at[me], p1_recv.at[me // 8]).start()
     for i in range(1, 4):
         block_copy(me // 4 * 4 + (me + i) % 4).start()
@@ -68,7 +91,6 @@
     @pl.loop(1, 32)
     def _(k):
         q = (me // 4 + k) % 32
-        turn(q)
         for i in range(4):
             block_copy(q * 4 + (me + i) % 4).start()
 
@@ -100,6 +122,8 @@
 
     def swap(value):
         return pltpu.roll(value, ROWS, 1)
+
+    mask_copy.wait()
 
     @pl.loop(0, TILES)
     def _(step):
@@ -284,9 +308,11 @@
     sums = pl.pallas_call(
         kernel,
         out_shape=jax.ShapeDtypeStruct((4, 2, 4, 4, 2, 32, TILE), BF16),
-        in_specs=[vmem, vmem, vmem, vmem, far],
+        in_specs=[far, far, vmem, vmem, far],
         out_specs=far,
         scratch_shapes=[
+            pltpu.VMEM(data.shape, BF16),
+            pltpu.VMEM(fill_mask.shape, jnp.int32),
             pltpu.VMEM((DEVICES, ROWS, 128), BF16),
             pltpu.VMEM((DEVICES, ROWS, 128), BF16),
             pltpu.VMEM((TILES, 2, 2, ROWS, 256), BF16),
@@ -302,9 +328,10 @@
             pltpu.SMEM((2, SLOTS, TILES), jnp.int32),
             dma(()), dma((16,)), dma((3,)), dma((3,)), dma((2,)), dma(()), dma((2, 4)), dma(()), dma((2,)),
             dma((3, 2)), dma((3, 2)), dma((3, 2)), dma((3, 2)), dma((4, 2)), dma((4, 2)), dma(()), dma((4,)),
+            dma((2,)), pltpu.SemaphoreType.REGULAR((3,)),
         ],
         compiler_params=pltpu.CompilerParams(
-            has_side_effects=True, vmem_limit_bytes=63 * 1024 * 1024
+            collective_id=1, has_side_effects=True, vmem_limit_bytes=63 * 1024 * 1024
         ),
         cost_estimate=pl.CostEstimate(
             flops=17_000_000_000, bytes_accessed=12_000_000, transcendentals=0

time: 206 us -> 201 us (0.976)
  Pallas kernels: 199 us -> 193 us
    pallas_call x1, Pallas kernels: 199 us -> 193 us  [local(): pl.pallas_call(kernel, out_shape=jax.ShapeDtypeStruct((4, 2, 4, 4, 2, 32,...]
where the time goes in v3:
time: 201 us
  Pallas kernels  193 us (96%)
  other arithmetic  7.22 us (4%)
    pallas_call x1, Pallas kernels, local(): pl.pallas_call(kernel, out_shape=jax.ShapeDtypeStruct((4, 2, 4, 4, 2, 32,...  193 us
    add x1, other arithmetic, local(): total = total + sums[d].astype(F32)  7.22 us

profile of v3, /device:TPU:10, one launch (start us, length us, event | category | flops | bytes accessed | tf_op | source)
XLA Modules:
  0.0 200.5 jit_solution(1397105776831918558)
XLA Ops:
  0.0 193.3 %shard_map.55 = bf16[4,2,4,4,2,32,512]{6,5,4,3,2,1,0:T(8,128)(2,1)} custom-call(bf16[2,64,8192]{2,1,0:T(8,128)(2,1)} %data_far.1, s32[64,8192]{1,0:T(8,128)} %mask_far.1, f32[64,128]{1,0:T(8,128)} %bitcast.4, s32[1,2]{1,0:T(1,128)} %bitcast.6, s32[2,8,16]{2,1,0:T(8,128)} %bitcast.5), custom_call_target="tpu_custom_call" | custom-call | flops 16999999488 | bytes 12000000 | tf_op jit(solution)/shard_map/pallas_call | solution.py:308
  193.3 7.2 %convert_add_fusion = f32[1,2,4,4,2,32,512]{6,5,4,3,2,1,0:T(8,128)} fusion(bf16[4,2,4,4,2,32,512]{6,5,4,3,2,1,0:T(8,128)(2,1)} %shard_map.55), kind=kLoop, calls=%fused_computation | loop fusion | flops 7340032 | bytes 12582912 | tf_op jit(solution)/shard_map/add | solution.py:342

commit v4 on v3

--- a/solution.py
+++ b/solution.py
@@ -18,9 +18,9 @@
 def kernel(
     data_far, mask_far, gain, lens, aperture,
     c_in,
-    data, mask, xt, recv, wb, a_out, a0, a1, a2, a3, b0, b1, b2, b3, c_out, lens_own, lens_all, lens_s, lists,
+    data, mask, xt, recv, wb, a_out, a0, a1, a2, a3, b0, b1, b2, b3, c_out, relay, lens_own, lens_all, lens_s, lists,
     p1_send, p1_recv, l_send, l_recv, l_copy, a2_send, a2_recv, b2_send, b2_recv,
-    a3_send, a3_recv, b3_send, b3_recv, s_send, s_recv, c_send, c_recv, in_copy, met,
+    a3_send, a3_recv, b3_send, b3_recv, s_send, s_recv, c_send, c_recv, r_recv, in_copy, met,
 ):
     src, rcv = lax.axis_index("src"), lax.axis_index("rcv")
     y, core = src // 2, src % 2
@@ -233,19 +233,48 @@
                 wide = jnp.concatenate([upper, left], axis=0)
                 term = jnp.dot(wide, right, preferred_element_type=F32)
                 total = term if total is None else total + term
-            place = (left_stage * 4 + right_stage) * 4 + step
-            c_out[place] = total.astype(BF16).reshape(2, 4, 32, 256)
-            columns = pl.ds(pl.multiple_of(yy % 2 * 256, 256), 256)
-            target = c_in.at[d, :, piece, :, half, :, columns]
+            h = yy % 2
+            index = left_stage * 2 + ea
+            held = c_out.at[index, d, h]
+            held[...] = total.astype(BF16).reshape(2, 4, 32, 256)
+            target = sum_place(d, piece, half, h)
 
             @pl.when(d == 0)
             def _():
-                pltpu.make_async_copy(c_out.at[place], target, c_recv.at[0]).start()
-
-            @pl.when(d != 0)
-            def _():
-                remote(c_out.at[place], target, c_send, c_recv.at[d],
+                pltpu.make_async_copy(held, target, c_recv.at[0]).start()
+
+            @pl.when(d == 2)
+            def _():
+                for way in range(2):
+                    remote(held.at[:, pl.ds(2 * way, 2)], relay.at[index, way, h],
+                           c_send, r_recv.at[index, way, h],
+                           device(y, core, x, (z + 3 - 2 * way) % 4)).start()
+
+            @pl.when(d % 2 == 1)
+            def _():
+                rows = pl.ds(3 - d, 2)
+                remote(held.at[:, rows], target.at[:, rows], c_send, c_recv.at[d // 2 + 1],
                        device(y, core, x, column)).start()
+
+    def sum_place(d, piece, half, h):
+        columns = pl.ds(pl.multiple_of(h * 256, 256), 256)
+        return c_in.at[(d + 1) // 2, :, piece, :, half, :, columns]
+
+    def finish(first, last, h):
+        @pl.loop(2 * first, 2 * last)
+        def _(step):
+            index, way = step // 2, step % 2
+            stage, e = index // 2, index % 2
+            near = jnp.logical_or(stage == 1, stage == 2)
+            piece = (x + jnp.where(near, 3 - 2 * e, stage // 3 * 2)) % 4
+            half = jnp.where(stage == 2, 1 - e, e)
+            d = 2 * way + 1
+            wait_on(relay.at[index, way, h], r_recv.at[index, way, h])
+            rows = pl.ds(2 * way, 2)
+            held = c_out.at[index, d, h, :, rows]
+            held[...] = (held[...].astype(F32) + relay[index, way, h].astype(F32)).astype(BF16)
+            remote(held, sum_place(d, piece, half, h).at[:, rows], c_send, c_recv.at[way + 1],
+                   device(y, core, x, (z - d + 4) % 4)).start()
 
     for e in range(2):
         wait_on(right_half(0, e), b2_recv.at[e])
@@ -268,6 +297,7 @@
     for e in range(2):
         sibling_copy(0, e).wait_recv()
     units(0, 0)
+    soon, late = 1 - y % 2, y % 2
     for stage in range(1, 4):
         for e in range(2):
             wait_on(right_half(stage, e), b3_recv.at[stage - 1, e])
@@ -278,12 +308,23 @@
             wait_on(left_half(stage, e), a3_recv.at[stage - 1, e])
             if stage == 1:
                 left_copy(3, e).start()
-        for earlier in range(stage):
-            units(stage, earlier)
+        units(stage, 0)
+        if stage == 2:
+            units(2, 1)
         for e in range(2):
             sibling_copy(stage, e).wait_recv()
-        for earlier in range(stage + 1):
+        for earlier in range(stage):
             units(earlier, stage)
+        if stage < 3:
+            units(stage, stage)
+        if stage == 2:
+            finish(0, 6, soon)
+    units(3, 1)
+    finish(0, 6, late)
+    units(3, 2)
+    units(3, 3)
+    finish(6, 8, soon)
+    finish(6, 8, late)
 
     wait_on(xt.at[pl.ds(0, DEVICES - 1)], p1_send)
     wait_on(wb.at[pl.ds(0, TILES - 1)], b2_send)
@@ -296,9 +337,9 @@
         for stage in range(1, 4):
             left_copy(stage, e).wait_send()
             right_copy(stage, e).wait_send()
-    wait_on(c_out.at[pl.ds(0, 48)], c_send)
-    for d in range(4):
-        wait_on(c_in.at[d], c_recv.at[d])
+    wait_on(c_out.at[pl.ds(0, 6)], c_send)
+    for side in range(3):
+        wait_on(c_in.at[side], c_recv.at[side])
 
 
 def local(data, fill_mask, obliquity, aperture, lengths):
@@ -307,7 +348,7 @@
     dma = pltpu.SemaphoreType.DMA
     sums = pl.pallas_call(
         kernel,
-        out_shape=jax.ShapeDtypeStruct((4, 2, 4, 4, 2, 32, TILE), BF16),
+        out_shape=jax.ShapeDtypeStruct((3, 2, 4, 4, 2, 32, TILE), BF16),
         in_specs=[far, far, vmem, vmem, far],
         out_specs=far,
         scratch_shapes=[
@@ -321,13 +362,15 @@
         + [pltpu.VMEM((2, TILES + 1, 4, 32, 256), BF16)] * 4
         + [pltpu.VMEM((2, 4, 2, 2, 2, 2, ROWS, 256), BF16)] * 4
         + [
-            pltpu.VMEM((64, 2, 4, 32, 256), BF16),
+            pltpu.VMEM((8, 4, 2, 2, 4, 32, 256), BF16),
+            pltpu.VMEM((8, 2, 2, 2, 2, 32, 256), BF16),
             pltpu.VMEM((8, 128), jnp.int32),
             pltpu.VMEM((4, 8, 128), jnp.int32),
             pltpu.SMEM((4, 8, 128), jnp.int32),
             pltpu.SMEM((2, SLOTS, TILES), jnp.int32),
             dma(()), dma((16,)), dma((3,)), dma((3,)), dma((2,)), dma(()), dma((2, 4)), dma(()), dma((2,)),
-            dma((3, 2)), dma((3, 2)), dma((3, 2)), dma((3, 2)), dma((4, 2)), dma((4, 2)), dma(()), dma((4,)),
+            dma((3, 2)), dma((3, 2)), dma((3, 2)), dma((3, 2)), dma((4, 2)), dma((4, 2)), dma(()), dma((3,)),
+            dma((8, 2, 2)),
             dma((2,)), pltpu.SemaphoreType.REGULAR((3,)),
         ],
         compiler_params=pltpu.CompilerParams(
@@ -338,8 +381,8 @@
         ),
     )(data, fill_mask, obliquity.reshape(64, 128), lengths.T, jnp.swapaxes(aperture, 1, 2))
     total = sums[0].astype(F32)
-    for d in range(1, 4):
-        total = total + sums[d].astype(F32)
+    for side in range(1, 3):
+        total = total + sums[side].astype(F32)
     return total.reshape(2, 2 * TILE, TILE)
 
 

time: 201 us -> 184 us (0.915)
  Pallas kernels: 193 us -> 177 us
    pallas_call x1, Pallas kernels: 193 us -> 177 us  [local(): pl.pallas_call(kernel, out_shape=jax.ShapeDtypeStruct((3, 2, 4, 4, 2, 32,...]
where the time goes in v4:
time: 184 us
  Pallas kernels  177 us (96%)
  other arithmetic  6.12 us (3%)
    pallas_call x1, Pallas kernels, local(): pl.pallas_call(kernel, out_shape=jax.ShapeDtypeStruct((3, 2, 4, 4, 2, 32,...  177 us
    add x1, other arithmetic, local(): total = total + sums[side].astype(F32)  6.12 us

profile of v4, /device:TPU:10, one launch (start us, length us, event | category | flops | bytes accessed | tf_op | source)
XLA Modules:
  0.0 183.6 jit_solution(9164547531232506848)
XLA Ops:
  0.0 177.5 %shard_map.55 = bf16[3,2,4,4,2,32,512]{6,5,4,3,2,1,0:T(8,128)(2,1)} custom-call(bf16[2,64,8192]{2,1,0:T(8,128)(2,1)} %data_far.1, s32[64,8192]{1,0:T(8,128)} %mask_far.1, f32[64,128]{1,0:T(8,128)} %bitcast.4, s32[1,2]{1,0:T(1,128)} %bitcast.6, s32[2,8,16]{2,1,0:T(8,128)} %bitcast.5), custom_call_target="tpu_custom_call" | custom-call | flops 16999999488 | bytes 12000000 | tf_op jit(solution)/shard_map/pallas_call | solution.py:349
  177.5 6.1 %convert_add_fusion = f32[1,2,4,4,2,32,512]{6,5,4,3,2,1,0:T(8,128)} fusion(bf16[3,2,4,4,2,32,512]{6,5,4,3,2,1,0:T(8,128)(2,1)} %shard_map.55), kind=kLoop, calls=%fused_computation | loop fusion | flops 5242880 | bytes 10485760 | tf_op jit(solution)/shard_map/add | solution.py:385

commit v5 on v4

--- a/solution.py
+++ b/solution.py
@@ -10,6 +10,7 @@
 TILES = 16
 ROWS = 64
 DEVICES = 128
+STRIDE = 5
 MESH = pl.DeviceIdType.MESH
 F32 = jnp.float32
 BF16 = jnp.bfloat16
@@ -49,10 +50,6 @@
     list_copy.start()
 
     barrier = pltpu.get_barrier_semaphore()
-    along_x = [device(y, core, (x + k) % 4, z) for k in range(1, 4)]
-    along_y = [device((y + k) % 4, core, x, z) for k in range(1, 4)]
-    along_z = [device(y, core, x, (z + k) % 4) for k in range(1, 4)]
-    sibling = [device(y, 1 - core, x, z)]
 
     def tell(semaphore, others):
         for other in others:
@@ -66,33 +63,29 @@
                 block = data[:, :, pl.ds(pl.multiple_of(q * 256, 256), 256)].reshape(128, 256)
                 xt[pl.ds(q * 4, 4)] = block.T.reshape(4, ROWS, 128)
 
-    tell(barrier, along_x + along_y + along_z + sibling)
+    along_yz = [device((y + k // 4) % 4, core, x, (z + k) % 4) for k in range(1, 16)]
+    across = [device(y, (core + k // 4) % 2, (x + k) % 4, z) for k in range(1, 8)]
+    tell(barrier, along_yz + across)
     data_copy.wait()
-    turn(0, 4)
-    pl.semaphore_wait(barrier, 10)
-    tell(met.at[0], along_x)
-    turn(4, 8)
-    pl.semaphore_wait(met.at[0], 3)
-    tell(met.at[1], along_y)
-    turn(8, 12)
-    pl.semaphore_wait(met.at[1], 3)
-    tell(met.at[2], sibling)
-    turn(12, 16)
-    pl.semaphore_wait(met.at[2], 1)
+    turn(0, 8)
+    pl.semaphore_wait(barrier, 22)
+    tell(met, across)
+    turn(8, 16)
+    pl.semaphore_wait(met, 7)
 
     def block_copy(target):
         return remote(xt.at[target], recv.at[me], p1_send, p1_recv.at[me // 8],
                       (target // 16, target % 16))
 
     pltpu.make_async_copy(xt.at[me], recv.at[me], p1_recv.at[me // 8]).start()
-    for i in range(1, 4):
-        block_copy(me // 4 * 4 + (me + i) % 4).start()
-
-    @pl.loop(1, 32)
-    def _(k):
-        q = (me // 4 + k) % 32
-        for i in range(4):
-            block_copy(q * 4 + (me + i) % 4).start()
+    for i in range(1, 8):
+        block_copy(me // 8 * 8 + (me + i) % 8).start()
+
+    @pl.loop(1, TILES)
+    def _(step):
+        tile = (me // 8 + STRIDE * step) % TILES
+        for i in range(8):
+            block_copy(tile * 8 + (me + i) % 8).start()
 
     lens_own[0:1, :] = jnp.broadcast_to(lens[:, 0:1], (1, 128))
     lens_own[1:2, :] = jnp.broadcast_to(lens[:, 1:2], (1, 128))
@@ -127,7 +120,7 @@
 
     @pl.loop(0, TILES)
     def _(step):
-        tile = (me // 8 - step - 1 + x % 2 + TILES) % TILES
+        tile = (me // 8 + (TILES - STRIDE) * step) % TILES
         group = recv.at[pl.ds(tile * 8, 8)]
         wait_on(group, p1_recv.at[tile])
         filled = []
@@ -348,9 +341,9 @@
     dma = pltpu.SemaphoreType.DMA
     sums = pl.pallas_call(
         kernel,
-        out_shape=jax.ShapeDtypeStruct((3, 2, 4, 4, 2, 32, TILE), BF16),
+        out_shape=pltpu.VMEM((3, 2, 4, 4, 2, 32, TILE), BF16),
         in_specs=[far, far, vmem, vmem, far],
-        out_specs=far,
+        out_specs=vmem,
         scratch_shapes=[
             pltpu.VMEM(data.shape, BF16),
             pltpu.VMEM(fill_mask.shape, jnp.int32),
@@ -371,10 +364,10 @@
             dma(()), dma((16,)), dma((3,)), dma((3,)), dma((2,)), dma(()), dma((2, 4)), dma(()), dma((2,)),
             dma((3, 2)), dma((3, 2)), dma((3, 2)), dma((3, 2)), dma((4, 2)), dma((4, 2)), dma(()), dma((3,)),
             dma((8, 2, 2)),
-            dma((2,)), pltpu.SemaphoreType.REGULAR((3,)),
+            dma((2,)), pltpu.SemaphoreType.REGULAR,
         ],
         compiler_params=pltpu.CompilerParams(
-            collective_id=1, has_side_effects=True, vmem_limit_bytes=63 * 1024 * 1024
+            collective_id=1, has_side_effects=True, vmem_limit_bytes=50 * 1024 * 1024
         ),
         cost_estimate=pl.CostEstimate(
             flops=17_000_000_000, bytes_accessed=12_000_000, transcendentals=0

time: 184 us -> 176 us (0.957); the launches traced: 184 us -> 173 us
  Pallas kernels: 177 us -> 170 us
  other arithmetic: 6.12 us -> 3.26 us
    pallas_call x1, Pallas kernels: 177 us -> 170 us  [local(): pl.pallas_call(kernel, out_shape=pltpu.VMEM((3, 2, 4, 4, 2, 32, TILE), BF...]
    add x1, other arithmetic: 6.12 us -> 3.26 us  [local(): total = total + sums[side].astype(F32)]
where the time goes in v5:
time: 176 us; the launch traced here: 173 us
  Pallas kernels  170 us (97%)
  other arithmetic  3.26 us (2%)
    pallas_call x1, Pallas kernels, local(): pl.pallas_call(kernel, out_shape=pltpu.VMEM((3, 2, 4, 4, 2, 32, TILE), BF...  170 us

profile of v5, /device:TPU:10, one launch (start us, length us, event | category | flops | bytes accessed | tf_op | source)
XLA Modules:
  0.0 173.4 jit_solution(5721709101252009249)
XLA Ops:
  0.0 170.1 %shard_map.55 = bf16[3,2,4,4,2,32,512]{6,5,4,3,2,1,0:T(8,128)(2,1)S(1)} custom-call(bf16[2,64,8192]{2,1,0:T(8,128)(2,1)} %data_far.1, s32[64,8192]{1,0:T(8,128)} %mask_far.1, f32[64,128]{1,0:T(8,128)} %bitcast.4, s32[1,2]{1,0:T(1,128)} %bitcast.6, s32[2,8,16]{2,1,0:T(8,128)} %bitcast.5), custom_call_target="tpu_custom_call" | custom-call | flops 16999999488 | bytes 12000000 | tf_op jit(solution)/shard_map/pallas_call | solution.py:342
  170.1 3.3 %convert_add_fusion = f32[1,2,4,4,2,32,512]{6,5,4,3,2,1,0:T(8,128)} fusion(bf16[3,2,4,4,2,32,512]{6,5,4,3,2,1,0:T(8,128)(2,1)S(1)} %shard_map.55), kind=kLoop, calls=%fused_computation | loop fusion | flops 5242880 | bytes 10485760 | tf_op jit(solution)/shard_map/add | solution.py:378

commit v6 on v5

--- a/solution.py
+++ b/solution.py
@@ -18,8 +18,8 @@
 
 def kernel(
     data_far, mask_far, gain, lens, aperture,
-    c_in,
-    data, mask, xt, recv, wb, a_out, a0, a1, a2, a3, b0, b1, b2, b3, c_out, relay, lens_own, lens_all, lens_s, lists,
+    mine, c_in,
+    data, mask, xt, recv, wb, a_out, a0, a1, a2, a3, b0, b1, b2, b3, c_out, relay, kept, lens_own, lens_all, lens_s, lists,
     p1_send, p1_recv, l_send, l_recv, l_copy, a2_send, a2_recv, b2_send, b2_recv,
     a3_send, a3_recv, b3_send, b3_recv, s_send, s_recv, c_send, c_recv, r_recv, in_copy, met,
 ):
@@ -229,12 +229,21 @@
             h = yy % 2
             index = left_stage * 2 + ea
             held = c_out.at[index, d, h]
-            held[...] = total.astype(BF16).reshape(2, 4, 32, 256)
-            target = sum_place(d, piece, half, h)
+            total = total.reshape(2, 4, 32, 256)
+            held[...] = total.astype(BF16)
 
             @pl.when(d == 0)
             def _():
-                pltpu.make_async_copy(held, target, c_recv.at[0]).start()
+                columns = pl.ds(pl.multiple_of(h * 256, 256), 256)
+                mine[:, piece, :, half, :, columns] = total
+
+            @pl.when(d == 1)
+            def _():
+                kept[index, 0, h] = total[:, :2]
+
+            @pl.when(d == 3)
+            def _():
+                kept[index, 1, h] = total[:, 2:]
 
             @pl.when(d == 2)
             def _():
@@ -246,12 +255,13 @@
             @pl.when(d % 2 == 1)
             def _():
                 rows = pl.ds(3 - d, 2)
-                remote(held.at[:, rows], target.at[:, rows], c_send, c_recv.at[d // 2 + 1],
+                target = sum_place(d // 2, piece, half, h).at[:, rows]
+                remote(held.at[:, rows], target, c_send, c_recv.at[d // 2],
                        device(y, core, x, column)).start()
 
-    def sum_place(d, piece, half, h):
+    def sum_place(way, piece, half, h):
         columns = pl.ds(pl.multiple_of(h * 256, 256), 256)
-        return c_in.at[(d + 1) // 2, :, piece, :, half, :, columns]
+        return c_in.at[way, :, piece, :, half, :, columns]
 
     def finish(first, last, h):
         @pl.loop(2 * first, 2 * last)
@@ -265,18 +275,18 @@
             wait_on(relay.at[index, way, h], r_recv.at[index, way, h])
             rows = pl.ds(2 * way, 2)
             held = c_out.at[index, d, h, :, rows]
-            held[...] = (held[...].astype(F32) + relay[index, way, h].astype(F32)).astype(BF16)
-            remote(held, sum_place(d, piece, half, h).at[:, rows], c_send, c_recv.at[way + 1],
+            held[...] = (kept[index, way, h] + relay[index, way, h].astype(F32)).astype(BF16)
+            remote(held, sum_place(way, piece, half, h).at[:, rows], c_send, c_recv.at[way],
                    device(y, core, x, (z - d + 4) % 4)).start()
 
+    for e in range(2):
+        for part in range(4):
+            wait_on(a0.at[e, pl.ds(0, TILES), part], a2_recv.at[e, part])
+        left_copy(1, e).start()
     for e in range(2):
         wait_on(right_half(0, e), b2_recv.at[e])
         right_copy(1, e).start()
         sibling_copy(0, e).start()
-    for e in range(2):
-        for part in range(4):
-            wait_on(a0.at[e, pl.ds(0, TILES), part], a2_recv.at[e, part])
-        left_copy(1, e).start()
     for e in range(2):
         right_copy(2, e).start()
         left_copy(2, e).start()
@@ -331,19 +341,21 @@
             left_copy(stage, e).wait_send()
             right_copy(stage, e).wait_send()
     wait_on(c_out.at[pl.ds(0, 6)], c_send)
-    for side in range(3):
-        wait_on(c_in.at[side], c_recv.at[side])
+    for way in range(2):
+        wait_on(c_in.at[way], c_recv.at[way])
 
 
 def local(data, fill_mask, obliquity, aperture, lengths):
     vmem = pl.BlockSpec(memory_space=pltpu.VMEM)
     far = pl.BlockSpec(memory_space=pl.ANY)
     dma = pltpu.SemaphoreType.DMA
-    sums = pl.pallas_call(
+    mine, sums = pl.pallas_call(
         kernel,
-        out_shape=pltpu.VMEM((3, 2, 4, 4, 2, 32, TILE), BF16),
+        out_shape=(
+            pltpu.VMEM((2, 4, 4, 2, 32, TILE), F32), pltpu.VMEM((2, 2, 4, 4, 2, 32, TILE), BF16)
+        ),
         in_specs=[far, far, vmem, vmem, far],
-        out_specs=vmem,
+        out_specs=(vmem, vmem),
         scratch_shapes=[
             pltpu.VMEM(data.shape, BF16),
             pltpu.VMEM(fill_mask.shape, jnp.int32),
@@ -357,25 +369,24 @@
         + [
             pltpu.VMEM((8, 4, 2, 2, 4, 32, 256), BF16),
             pltpu.VMEM((8, 2, 2, 2, 2, 32, 256), BF16),
+            pltpu.VMEM((8, 2, 2, 2, 2, 32, 256), F32),
             pltpu.VMEM((8, 128), jnp.int32),
             pltpu.VMEM((4, 8, 128), jnp.int32),
             pltpu.SMEM((4, 8, 128), jnp.int32),
             pltpu.SMEM((2, SLOTS, TILES), jnp.int32),
             dma(()), dma((16,)), dma((3,)), dma((3,)), dma((2,)), dma(()), dma((2, 4)), dma(()), dma((2,)),
-            dma((3, 2)), dma((3, 2)), dma((3, 2)), dma((3, 2)), dma((4, 2)), dma((4, 2)), dma(()), dma((3,)),
+            dma((3, 2)), dma((3, 2)), dma((3, 2)), dma((3, 2)), dma((4, 2)), dma((4, 2)), dma(()), dma((2,)),
             dma((8, 2, 2)),
             dma((2,)), pltpu.SemaphoreType.REGULAR,
         ],
         compiler_params=pltpu.CompilerParams(
-            collective_id=1, has_side_effects=True, vmem_limit_bytes=50 * 1024 * 1024
+            collective_id=1, has_side_effects=True, vmem_limit_bytes=54 * 1024 * 1024
         ),
         cost_estimate=pl.CostEstimate(
             flops=17_000_000_000, bytes_accessed=12_000_000, transcendentals=0
         ),
     )(data, fill_mask, obliquity.reshape(64, 128), lengths.T, jnp.swapaxes(aperture, 1, 2))
-    total = sums[0].astype(F32)
-    for side in range(1, 3):
-        total = total + sums[side].astype(F32)
+    total = mine + sums[0].astype(F32) + sums[1].astype(F32)
     return total.reshape(2, 2 * TILE, TILE)
 
 

time: 176 us -> 175 us (level)
  no operation moved by 1% of the time
where the time goes in v6:
time: 175 us; the launch traced here: 173 us
  Pallas kernels  170 us (97%)
  other arithmetic  3.27 us (2%)
    pallas_call x1, Pallas kernels, local(): pl.pallas_call(kernel, out_shape=(pltpu.VMEM((2, 4, 4, 2, 32, TILE), F32)...  170 us

profile of v6, /device:TPU:10, one launch (start us, length us, event | category | flops | bytes accessed | tf_op | source)
XLA Modules:
  0.0 173.2 jit_solution(526181849686829047)
XLA Ops:
  0.0 169.9 %shard_map.55 = (f32[2,4,4,2,32,512]{5,4,3,2,1,0:T(8,128)S(1)}, bf16[2,2,4,4,2,32,512]{6,5,4,3,2,1,0:T(8,128)(2,1)S(1)}) custom-call(bf16[2,64,8192]{2,1,0:T(8,128)(2,1)} %data_far.1, s32[64,8192]{1,0:T(8,128)} %mask_far.1, f32[64,128]{1,0:T(8,128)} %bitcast.10, s32[1,2]{1,0:T(1,128)} %bitcast.12, s32[2,8,16]{2,1,0:T(8,128)} %bitcast.11), custom_call_target="tpu_custom_call" | custom-call | flops 16999999488 | bytes 12000000 | tf_op jit(solution)/shard_map/pallas_call | solution.py:352
  169.9 3.3 %convert_add_fusion = f32[2,4,4,2,32,512]{5,4,3,2,1,0:T(8,128)} fusion(f32[2,4,4,2,32,512]{5,4,3,2,1,0:T(8,128)S(1)} %get-tuple-element.7, bf16[2,2,4,4,2,32,512]{6,5,4,3,2,1,0:T(8,128)(2,1)S(1)} %get-tuple-element.8), kind=kLoop, calls=%fused_computation | loop fusion | flops 4194304 | bytes 12582912 | tf_op jit(solution)/shard_map/add | solution.py:389

commit v7 on v6

--- a/solution.py
+++ b/solution.py
@@ -155,11 +155,11 @@
 
             @pl.when(mine)
             def _():
-                pltpu.make_async_copy(source, target, b2_recv.at[d // 2]).start()
+                pltpu.make_async_copy(source, target, b2_recv.at[d // 2, y]).start()
 
             @pl.when(jnp.logical_not(mine))
             def _():
-                remote(source, target, b2_send, b2_recv.at[d // 2],
+                remote(source, target, b2_send, b2_recv.at[d // 2, y],
                        device(to_y, core, tile // 4, z)).start()
         for k in range(1, 4):
             to = (z + k) % 4
@@ -279,13 +279,20 @@
             remote(held, sum_place(way, piece, half, h).at[:, rows], c_send, c_recv.at[way],
                    device(y, core, x, (z - d + 4) % 4)).start()
 
+    for i in range(4):
+        for e in range(2):
+            part = (z + i) % 4
+            source = a0.at[e, pl.ds(0, TILES), part]
+            wait_on(source, a2_recv.at[e, part])
+            remote(source, a1.at[e, pl.ds(0, TILES), part], a3_send.at[0, e], a3_recv.at[0, e],
+                   device(y, core, (x + 1 + 2 * e) % 4, z)).start()
+        for e in range(2):
+            part = (y + i) % 4
+            source = b0.at[e, part, core]
+            wait_on(source, b2_recv.at[e, part])
+            remote(source, b1.at[e, part, core], b3_send.at[0, e], b3_recv.at[0, e],
+                   device((y + 1 + 2 * e) % 4, core, x, z)).start()
     for e in range(2):
-        for part in range(4):
-            wait_on(a0.at[e, pl.ds(0, TILES), part], a2_recv.at[e, part])
-        left_copy(1, e).start()
-    for e in range(2):
-        wait_on(right_half(0, e), b2_recv.at[e])
-        right_copy(1, e).start()
         sibling_copy(0, e).start()
     for e in range(2):
         right_copy(2, e).start()
@@ -374,7 +381,7 @@
             pltpu.VMEM((4, 8, 128), jnp.int32),
             pltpu.SMEM((4, 8, 128), jnp.int32),
             pltpu.SMEM((2, SLOTS, TILES), jnp.int32),
-            dma(()), dma((16,)), dma((3,)), dma((3,)), dma((2,)), dma(()), dma((2, 4)), dma(()), dma((2,)),
+            dma(()), dma((16,)), dma((3,)), dma((3,)), dma((2,)), dma(()), dma((2, 4)), dma(()), dma((2, 4)),
             dma((3, 2)), dma((3, 2)), dma((3, 2)), dma((3, 2)), dma((4, 2)), dma((4, 2)), dma(()), dma((2,)),
             dma((8, 2, 2)),
             dma((2,)), pltpu.SemaphoreType.REGULAR,

time: 175 us -> 174 us (level)
  no operation moved by 1% of the time
where the time goes in v7:
time: 174 us; the launch traced here: 173 us
  Pallas kernels  169 us (97%)
  other arithmetic  3.27 us (2%)
    pallas_call x1, Pallas kernels, local(): pl.pallas_call(kernel, out_shape=(pltpu.VMEM((2, 4, 4, 2, 32, TILE), F32)...  169 us

profile of v7, /device:TPU:10, one launch (start us, length us, event | category | flops | bytes accessed | tf_op | source)
XLA Modules:
  0.0 172.8 jit_solution(3161622715117563783)
XLA Ops:
  0.0 169.5 %shard_map.55 = (f32[2,4,4,2,32,512]{5,4,3,2,1,0:T(8,128)S(1)}, bf16[2,2,4,4,2,32,512]{6,5,4,3,2,1,0:T(8,128)(2,1)S(1)}) custom-call(bf16[2,64,8192]{2,1,0:T(8,128)(2,1)} %data_far.1, s32[64,8192]{1,0:T(8,128)} %mask_far.1, f32[64,128]{1,0:T(8,128)} %bitcast.10, s32[1,2]{1,0:T(1,128)} %bitcast.12, s32[2,8,16]{2,1,0:T(8,128)} %bitcast.11), custom_call_target="tpu_custom_call" | custom-call | flops 16999999488 | bytes 12000000 | tf_op jit(solution)/shard_map/pallas_call | solution.py:359
  169.5 3.3 %convert_add_fusion = f32[2,4,4,2,32,512]{5,4,3,2,1,0:T(8,128)} fusion(f32[2,4,4,2,32,512]{5,4,3,2,1,0:T(8,128)S(1)} %get-tuple-element.7, bf16[2,2,4,4,2,32,512]{6,5,4,3,2,1,0:T(8,128)(2,1)S(1)} %get-tuple-element.8), kind=kLoop, calls=%fused_computation | loop fusion | flops 4194304 | bytes 12582912 | tf_op jit(solution)/shard_map/add | solution.py:396

commit v8 on v7

--- a/solution.py
+++ b/solution.py
@@ -329,12 +329,12 @@
             units(stage, stage)
         if stage == 2:
             finish(0, 6, soon)
+    units(3, 3)
+    finish(0, 6, late)
     units(3, 1)
-    finish(0, 6, late)
     units(3, 2)
-    units(3, 3)
+    finish(6, 8, late)
     finish(6, 8, soon)
-    finish(6, 8, late)
 
     wait_on(xt.at[pl.ds(0, DEVICES - 1)], p1_send)
     wait_on(wb.at[pl.ds(0, TILES - 1)], b2_send)

time: 174 us -> 174 us (level)
  no operation moved by 1% of the time
where the time goes in v8:
time: 174 us; the launch traced here: 173 us
  Pallas kernels  169 us (97%)
  other arithmetic  3.27 us (2%)
    pallas_call x1, Pallas kernels, local(): pl.pallas_call(kernel, out_shape=(pltpu.VMEM((2, 4, 4, 2, 32, TILE), F32)...  169 us

profile of v8, /device:TPU:10, one launch (start us, length us, event | category | flops | bytes accessed | tf_op | source)
XLA Modules:
  0.0 172.8 jit_solution(15820726805618938128)
XLA Ops:
  0.0 169.5 %shard_map.55 = (f32[2,4,4,2,32,512]{5,4,3,2,1,0:T(8,128)S(1)}, bf16[2,2,4,4,2,32,512]{6,5,4,3,2,1,0:T(8,128)(2,1)S(1)}) custom-call(bf16[2,64,8192]{2,1,0:T(8,128)(2,1)} %data_far.1, s32[64,8192]{1,0:T(8,128)} %mask_far.1, f32[64,128]{1,0:T(8,128)} %bitcast.10, s32[1,2]{1,0:T(1,128)} %bitcast.12, s32[2,8,16]{2,1,0:T(8,128)} %bitcast.11), custom_call_target="tpu_custom_call" | custom-call | flops 16999999488 | bytes 12000000 | tf_op jit(solution)/shard_map/pallas_call | solution.py:359
  169.5 3.3 %convert_add_fusion = f32[2,4,4,2,32,512]{5,4,3,2,1,0:T(8,128)} fusion(f32[2,4,4,2,32,512]{5,4,3,2,1,0:T(8,128)S(1)} %get-tuple-element.7, bf16[2,2,4,4,2,32,512]{6,5,4,3,2,1,0:T(8,128)(2,1)S(1)} %get-tuple-element.8), kind=kLoop, calls=%fused_computation | loop fusion | flops 4194304 | bytes 12582912 | tf_op jit(solution)/shard_map/add | solution.py:396
